TPU v7x, 512 devices: a whole 4x8x8 slice. The times are simulated.
512 devices in a mesh: seq: 32 (over z_lo, y, core), head: 16 (over z_hi, x).
Axes of the slice: x: 4, y: 8, z: 8 (z_hi: 4, z_lo: 2; z = z_hi * 2 + z_lo), core: 2. Of those that a mesh axis runs over, the one named last changes fastest.
Arguments:
- source_hidden: bfloat16 [8192, 2048], P('seq', 'head'), may hold values from -64 to 64
- target_hidden: bfloat16 [16384, 2048], P('seq', 'head'), may hold values from -64 to 64
- source_length: int32 [1], replicated, may hold values from 4096 to 8192
- target_length: int32 [1], replicated, may hold values from 8192 to 16384
- encoder_gain: float32 [2048], replicated, may hold values from 0.25 to 1.75
- query_weight: bfloat16 [2048, 2048], P(None, 'head'), may hold values from -1 to 1
- key_weight: bfloat16 [2048, 2048], P(None, 'head'), may hold values from -1 to 1
- value_weight: bfloat16 [2048, 2048], P(None, 'head'), may hold values from -0.5 to 0.5
- output_weight: bfloat16 [2048, 2048], P('head'), may hold values from -0.5 to 0.5
- final_gain: float32 [2048], replicated, may hold values from 0.25 to 1.75
- cross_query: bfloat16 [2048, 2048], P(None, 'head'), may hold values from -1 to 1
- cross_key: bfloat16 [2048, 2048], P(None, 'head'), may hold values from -1 to 1
- cross_value: bfloat16 [2048, 2048], P(None, 'head'), may hold values from -0.5 to 0.5
- cross_gain: float32 [2048], replicated, may hold values from 0.25 to 1.75
Outputs:
- encoder_out: bfloat16 [8192, 2048], P('seq', 'head')
- cross_context: bfloat16 [16384, 2048], P('seq', 'head')
All inputs are finite; a program needn't handle non-finite values.
Results may differ from a plain program's by a relative error of at most 0.03.
Values may be sent and summed in bfloat16 or wider, within the bound.
No kernel may reach another device: no remote copies, remote signals or barrier semaphores. Data moves between devices by JAX's collectives and lax.ppermute only.
A program may use at most 64 MiB of HBM per device.

v0:
```python
import math
import jax
import jax.numpy as jnp
from jax import lax
from jax.sharding import PartitionSpec as P

HD = 128
EPSILON = 1e-05
MASKED = -1e30


def layer_norm(hidden, scale_gain):
    floats = hidden.astype(jnp.float32)
    center = floats - jnp.mean(floats, axis=-1, keepdims=True)
    spread = jnp.mean(center * center, axis=-1, keepdims=True)
    return (center * lax.rsqrt(spread + EPSILON) * scale_gain).astype(jnp.bfloat16)


def project(normed, weight):
    return jnp.dot(normed, weight, preferred_element_type=jnp.float32).astype(jnp.bfloat16)


def make_fold(queries, key_limit):
    head_count = queries.shape[1] // HD
    row_count = queries.shape[0]
    grouped = queries.reshape(row_count, head_count, HD)

    def fold_keys(running, pieces, first_row):
        key_rows, value_rows = pieces
        key_count = key_rows.shape[0]
        block_size = math.gcd(key_count, 1024)

        def block_step(block_index, carried):
            running_max, denominator, context_sum = carried
            offset = block_index * block_size
            key_block = lax.dynamic_slice_in_dim(key_rows, offset, block_size, 0).reshape(
                block_size, head_count, HD
            )
            value_block = lax.dynamic_slice_in_dim(value_rows, offset, block_size, 0).reshape(
                block_size, head_count, HD
            )
            places = offset + lax.iota(jnp.int32, block_size)
            usable = (places < key_limit)[None, None, :]
            scores = jnp.einsum(
                "rhd,khd->hrk", grouped, key_block, preferred_element_type=jnp.float32
            ) * HD ** (-0.5)
            scores = jnp.where(usable, scores, MASKED)
            new_max = jnp.maximum(running_max, jnp.max(scores, axis=-1))
            weights = jnp.where(usable, jnp.exp(scores - new_max[:, :, None]), 0.0)
            rescale = jnp.exp(running_max - new_max)
            denominator = denominator * rescale + jnp.sum(weights, axis=-1)
            update = jnp.einsum(
                "hrk,khd->rhd",
                weights.astype(jnp.bfloat16),
                value_block,
                preferred_element_type=jnp.float32,
            )
            context_sum = context_sum * rescale.T[:, :, None] + update
            return (new_max, denominator, context_sum)

        return lax.fori_loop(0, key_count // block_size, block_step, running)

    initial = (
        jnp.full((head_count, row_count), MASKED, jnp.float32),
        jnp.zeros((head_count, row_count), jnp.float32),
        jnp.zeros((row_count, head_count, HD), jnp.float32),
    )
    return (fold_keys, initial)


def finish(running):
    running_max, denominator, context_sum = running
    row_count = context_sum.shape[0]
    return (context_sum / denominator.T[:, :, None]).reshape(row_count, -1)


def shards(
    source_hidden,
    target_hidden,
    source_length,
    target_length,
    encoder_gain,
    query_weight,
    key_weight,
    value_weight,
    output_weight,
    final_gain,
    cross_query,
    cross_key,
    cross_value,
    cross_gain,
):
    source_full, target_full = (
        lax.all_gather(source_hidden, "head", axis=1, tiled=True),
        lax.all_gather(target_hidden, "head", axis=1, tiled=True),
    )
    key_limit = source_length[0]
    source_norm = layer_norm(source_full, encoder_gain)
    queries = project(source_norm, query_weight)
    keys_local = project(source_norm, key_weight)
    values_local = project(source_norm, value_weight)
    folder, initial = make_fold(queries, key_limit)
    attended = folder(
        initial,
        (
            lax.all_gather(keys_local, "seq", axis=0, tiled=True),
            lax.all_gather(values_local, "seq", axis=0, tiled=True),
        ),
        jnp.int32(0),
    )
    encoder_context = finish(attended).astype(jnp.bfloat16)
    partial_sum = jnp.dot(encoder_context, output_weight, preferred_element_type=jnp.float32)
    share_sum = lax.psum_scatter(
        partial_sum.astype(jnp.bfloat16), "head", scatter_dimension=1, tiled=True
    ).astype(jnp.float32)
    encoder_out = (source_hidden.astype(jnp.float32) + share_sum).astype(jnp.bfloat16)
    encoder_full = lax.all_gather(encoder_out, "head", axis=1, tiled=True)
    encoder_final = layer_norm(encoder_full, final_gain)
    memory_keys = project(encoder_final, cross_key)
    memory_values = project(encoder_final, cross_value)
    target_norm = layer_norm(target_full, cross_gain)
    target_queries = project(target_norm, cross_query)
    cross_folder, cross_initial = make_fold(target_queries, key_limit)
    crossed = cross_folder(
        cross_initial,
        (
            lax.all_gather(memory_keys, "seq", axis=0, tiled=True),
            lax.all_gather(memory_values, "seq", axis=0, tiled=True),
        ),
        jnp.int32(0),
    )
    target_rows = target_hidden.shape[0]
    positions = lax.axis_index("seq") * target_rows + lax.iota(jnp.int32, target_rows)
    live_rows = (positions < target_length[0])[:, None]
    cross_context = jnp.where(live_rows, finish(crossed), 0.0).astype(jnp.bfloat16)
    return (encoder_out, cross_context)


def solution(mesh):
    in_specs = (
        P("seq", "head"),
        P("seq", "head"),
        P(),
        P(),
        P(),
        P(None, "head"),
        P(None, "head"),
        P(None, "head"),
        P("head", None),
        P(),
        P(None, "head"),
        P(None, "head"),
        P(None, "head"),
        P(),
    )
    out_specs = (P("seq", "head"), P("seq", "head"))
    return jax.shard_map(shards, mesh=mesh, in_specs=in_specs, out_specs=out_specs, check_vma=False)
```

profile of v0, /device:TPU:1, one launch (start us, length us, event | category | flops | bytes accessed | tf_op | source)
XLA Modules:
  0.0 650.4 jit_solution(5712484617599095575)
XLA Ops:
  8.0 68.6 %all-gather.8.cloned.1.call-done = bf16[256,2048]{1,0:T(8,128)(2,1)} async-done(((bf16[256,128]{1,0:T(8,128)(2,1)}), bf16[256,2048]{1,0:T(8,128)(2,1)}) %all-gather.8.cloned.1.call-update) | async-done | bytes 1048592 | tf_op jit(solution)/shard_map/all_gather | solution.py:94
  76.6 1.5 convert_reduce_fusion.2
  78.1 1.6 fusion.50
  83.0 63.3 %all-gather.10.cloned.1.call-done = bf16[8192,128]{1,0:T(8,128)(2,1)} async-done(((bf16[256,128]{1,0:T(8,128)(2,1)}), bf16[8192,128]{1,0:T(8,128)(2,1)}) %all-gather.10.cloned.1.call-update) | async-done | bytes 2097168 | tf_op jit(solution)/shard_map/all_gather | solution.py:106
  146.3 69.8 %all-gather.12.cloned.1.call-done = bf16[8192,128]{1,0:T(8,128)(2,1)} async-done(((bf16[256,128]{1,0:T(8,128)(2,1)}), bf16[8192,128]{1,0:T(8,128)(2,1)}) %all-gather.12.cloned.1.call-update) | async-done | bytes 2097168 | tf_op jit(solution)/shard_map/all_gather | solution.py:107
  216.1 29.3 %while.36 = (s32[]{:T(128)}, f32[1,256]{1,0:T(1,128)S(1)}, f32[1,256]{1,0:T(1,128)S(1)}, f32[256,1,128]{0,2,1:T(8,128)S(1)}, s32[]{:T(128)}, /*index=5*/bf16[819...) while((s32[]{:T(128)}, f32[1,256]{1,0:T(1,128)S(1)}, ...), condition=%wide.region_5.6_spmd.clone, body=%wide.region_2.5_spmd.clone.sunk | while | flops 136678656 | bytes 4018367 | solution.py:61
  240.3 1.4 fusion.100
  247.2 89.8 %reduce-scatter.4.cloned.1.call-done = bf16[128,256]{1,0:T(8,128)(2,1)} async-done(((bf16[2048,256]{1,0:T(8,128)(2,1)}), bf16[128,256]{1,0:T(8,128)(2,1)}) %reduce-scatter.4.cloned.1.call-update) | async-done | bytes 65552
  339.3 60.9 %all-gather.14.cloned.1.call-done = bf16[256,2048]{1,0:T(8,128)(2,1)} async-done(((bf16[256,128]{1,0:T(8,128)(2,1)}), bf16[256,2048]{1,0:T(8,128)(2,1)}) %all-gather.14.cloned.1.call-update) | async-done | bytes 1048592 | tf_op jit(solution)/shard_map/all_gather | solution.py:117
  400.2 1.5 convert_reduce_fusion.1
  401.8 1.7 fusion.47
  406.7 62.5 %all-gather.18.cloned.1.call-done = bf16[512,2048]{1,0:T(8,128)(2,1)} async-done(((bf16[512,128]{1,0:T(8,128)(2,1)}), bf16[512,2048]{1,0:T(8,128)(2,1)}) %all-gather.18.cloned.1.call-update) | async-done | bytes 2097168 | tf_op jit(solution)/shard_map/all_gather | solution.py:95
  469.2 2.1 convert_reduce_fusion
  473.0 64.2 %all-gather.20.cloned.1.call-done = bf16[8192,128]{1,0:T(8,128)(2,1)} async-done(((bf16[256,128]{1,0:T(8,128)(2,1)}), bf16[8192,128]{1,0:T(8,128)(2,1)}) %all-gather.20.cloned.1.call-update) | async-done | bytes 2097168 | tf_op jit(solution)/shard_map/all_gather | solution.py:128
  537.2 70.0 %all-gather.16.cloned.1.call-done = bf16[8192,128]{1,0:T(8,128)(2,1)} async-done(((bf16[256,128]{1,0:T(8,128)(2,1)}), bf16[8192,128]{1,0:T(8,128)(2,1)}) %all-gather.16.cloned.1.call-update) | async-done | bytes 2097168 | tf_op jit(solution)/shard_map/all_gather | solution.py:127
  607.1 35.5 %while.37 = (s32[]{:T(128)}, f32[1,512]{1,0:T(1,128)S(1)}, f32[1,512]{1,0:T(1,128)S(1)}, f32[512,1,128]{0,2,1:T(8,128)S(1)}, s32[]{:T(128)}, /*index=5*/bf16[819...) while((s32[]{:T(128)}, f32[1,512]{1,0:T(1,128)S(1)}, ...), condition=%wide.region_14.15_spmd.clone, body=%wide.region_11.14_spmd.clone.sunk | while | flops 275452416 | bytes 7508159 | solution.py:61
  607.8 1.4 fusion.103
  609.8 1.7 fusion.107
  612.2 1.4 fusion.103
  614.3 1.7 fusion.107
  616.7 1.4 fusion.103
  618.7 1.7 fusion.107
  621.1 1.4 fusion.103
  623.1 1.7 fusion.107
  625.5 1.4 fusion.103
  627.6 1.7 fusion.107
  630.0 1.4 fusion.103
  632.0 1.7 fusion.107
  634.4 1.4 fusion.103
  636.4 1.7 fusion.107
  638.8 1.4 fusion.103
  640.9 1.7 fusion.107
  (166 shorter events, 50.5 us)
Async XLA Ops:
  7.2 238.2 %copy-start = (bf16[128,2048]{1,0:T(8,128)(2,1)S(1)}, bf16[128,2048]{1,0:T(8,128)(2,1)}, u32[]{:S(2)}) copy-start(bf16[128,2048]{1,0:T(8,128)(2,1)} %param.26) | copy-start | bytes 1572868
  7.2 72.6 %copy-start.8 = (f32[2048]{0:T(1024)S(1)}, f32[2048]{0:T(1024)}, u32[]{:S(2)}) copy-start(f32[2048]{0:T(1024)} %param.22) | copy-start | bytes 24580
  7.2 69.4 %all-gather.8.cloned.1.call-start = ((), (), s32[]{:S(2)}) async-start(), calls=%async_computation.1 | async-start | bytes 1114112 | tf_op jit(solution)/shard_map/all_gather | solution.py:94
  7.9 72.3 %copy-start.4 = (bf16[2048,128]{1,0:T(8,128)(2,1)S(1)}, bf16[2048,128]{1,0:T(8,128)(2,1)}, u32[]{:S(2)}) copy-start(bf16[2048,128]{1,0:T(8,128)(2,1)} %param.24) | copy-start | bytes 1572868
  7.9 138.4 %all-gather.10.cloned.1.call-start = ((), (), s32[]{:S(2)}) async-start(), calls=%async_computation.2 | async-start | bytes 2162688 | tf_op jit(solution)/shard_map/all_gather | solution.py:106
  76.6 3.2 copy-start.1
  79.8 1.6 copy-start.5
  80.2 2.3 copy-start.6
  81.3 134.8 %all-gather.12.cloned.1.call-start = ((), (), s32[]{:S(2)}) async-start(), calls=%async_computation.3 | async-start | bytes 2162688 | tf_op jit(solution)/shard_map/all_gather | solution.py:107
  82.5 254.6 %reduce-scatter.4.cloned.1.call-start = ((), (), s32[]{:S(2)}) async-start(), calls=%async_computation.8 | async-start | bytes 1114112
  245.4 92.6 %copy-start.7 = (bf16[256,128]{1,0:T(8,128)(2,1)S(1)}, bf16[256,128]{1,0:T(8,128)(2,1)}, u32[]{:S(2)}) copy-start(bf16[256,128]{1,0:T(8,128)(2,1)} %param.18) | copy-start | bytes 196612
  247.2 156.3 %copy-start.9 = (bf16[2048,128]{1,0:T(8,128)(2,1)S(1)}, bf16[2048,128]{1,0:T(8,128)(2,1)}, u32[]{:S(2)}) copy-start(bf16[2048,128]{1,0:T(8,128)(2,1)} %param.30) | copy-start | bytes 1572868
  247.2 156.3 %copy-start.12 = (f32[2048]{0:T(1024)S(1)}, f32[2048]{0:T(1024)}, u32[]{:S(2)}) copy-start(f32[2048]{0:T(1024)} %param.27) | copy-start | bytes 24580
  247.2 153.0 %all-gather.14.cloned.1.call-start = ((), (), s32[]{:S(2)}) async-start(), calls=%async_computation.4 | async-start | bytes 1114112 | tf_op jit(solution)/shard_map/all_gather | solution.py:117
  338.7 130.5 %all-gather.18.cloned.1.call-start = ((), (), s32[]{:S(2)}) async-start(), calls=%async_computation.6 | async-start | bytes 2228224 | tf_op jit(solution)/shard_map/all_gather | solution.py:95
  339.3 197.9 %all-gather.20.cloned.1.call-start = ((), (), s32[]{:S(2)}) async-start(), calls=%async_computation.7 | async-start | bytes 2162688 | tf_op jit(solution)/shard_map/all_gather | solution.py:128
  400.2 3.3 copy-start.3
  401.8 3.0 copy-start.10
  404.7 202.4 %all-gather.16.cloned.1.call-start = ((), (), s32[]{:S(2)}) async-start(), calls=%async_computation.5 | async-start | bytes 2162688 | tf_op jit(solution)/shard_map/all_gather | solution.py:127
  469.2 2.2 copy-start.2
  469.2 2.9 copy-start.11
  469.2 2.9 copy-start.13
Sparse Core Ops, SparseCore 0:
  11.0 65.5 all-gather.7
  81.4 64.8 all-gather.9
  149.0 66.9 all-gather.11
  247.3 89.7 reduce-scatter.3
  340.9 59.2 all-gather.13
  403.5 65.6 all-gather.17
  471.6 65.5 all-gather.19
  540.1 66.9 all-gather.15
where the time goes:
time: 652 us; the launch traced here: 650 us
  waiting for transfers between devices  550 us (84%)
  matrix products  52.6 us (8%)
  other arithmetic  28.4 us (4%)
  between operations  15.1 us (2%)
    unnamed x9, waiting for transfers between devices  91.1 us
    all_gather x1, waiting for transfers between devices, shards(): lax.all_gather(memory_keys, 'seq', axis=0, tiled=True)  70 us
    all_gather x1, waiting for transfers between devices, shards(): lax.all_gather(values_local, 'seq', axis=0, tiled=True)  69.8 us
    all_gather x1, waiting for transfers between devices, shards(): lax.all_gather(source_hidden, 'head', axis=1, tiled=True)  68.6 us
    all_gather x1, waiting for transfers between devices, shards(): lax.all_gather(memory_values, 'seq', axis=0, tiled=True)  64.2 us
    all_gather x1, waiting for transfers between devices, shards(): lax.all_gather(keys_local, 'seq', axis=0, tiled=True)  63.3 us
    all_gather x1, waiting for transfers between devices, shards(): lax.all_gather(target_hidden, 'head', axis=1, tiled=True)  62.5 us
    all_gather x1, waiting for transfers between devices, shards(): encoder_full = lax.all_gather(encoder_out, 'head', axis=1, tiled=True)  60.9 us
  transfers between devices with their start and end apart: 8, of which 8 were waited for; matrix products, arithmetic and copies ran while one was open for 2% of the time, Pallas kernels for 0%

commit v1 on v0

--- a/solution.py
+++ b/solution.py
@@ -103,7 +103,12 @@
     attended = folder(
         initial,
         (
-            lax.all_gather(keys_local, "seq", axis=0, tiled=True),
+            jnp.concatenate(
+                lax.all_to_all(
+                    jnp.stack([keys_local for _ in range(lax.axis_size("seq"))], 0), "seq", 0, 0
+                ),
+                axis=0,
+            ),
             lax.all_gather(values_local, "seq", axis=0, tiled=True),
         ),
         jnp.int32(0),

time: 652 us -> 603 us (0.925)
  waiting for transfers between devices: 550 us -> 492 us
  starting transfers between devices: 0.32 us -> 8.19 us
    all_gather x1 -> x0, waiting for transfers between devices: 63.3 us -> none  [shards(): lax.all_gather(keys_local, 'seq', axis=0, tiled=True)]
    all_to_all x0 -> x1, waiting for transfers between devices: none -> 53.1 us  [shards(): lax.all_to_all(jnp.stack([keys_local for _ in range(lax.axis_size('seq'))...]
    all_gather x1, waiting for transfers between devices: 69.8 us -> 22.4 us  [shards(): lax.all_gather(values_local, 'seq', axis=0, tiled=True)]
    all_to_all x0 -> x1, starting transfers between devices: none -> 7.91 us  [shards(): lax.all_to_all(jnp.stack([keys_local for _ in range(lax.axis_size('seq'))...]
    unnamed x9 -> x8, waiting for transfers between devices: 91.1 us -> 90.6 us
where the time goes in v1:
time: 603 us; the launch traced here: 601 us
  waiting for transfers between devices  492 us (82%)
  matrix products  52 us (9%)
  other arithmetic  28.4 us (5%)
  between operations  15.1 us (3%)
  starting transfers between devices  8.19 us (1%)
    unnamed x8, waiting for transfers between devices  90.6 us
    all_gather x1, waiting for transfers between devices, shards(): lax.all_gather(memory_keys, 'seq', axis=0, tiled=True)  70 us
    all_gather x1, waiting for transfers between devices, shards(): lax.all_gather(source_hidden, 'head', axis=1, tiled=True)  68.7 us
    all_gather x1, waiting for transfers between devices, shards(): lax.all_gather(memory_values, 'seq', axis=0, tiled=True)  64 us
    all_gather x1, waiting for transfers between devices, shards(): lax.all_gather(target_hidden, 'head', axis=1, tiled=True)  62.5 us
    all_gather x1, waiting for transfers between devices, shards(): encoder_full = lax.all_gather(encoder_out, 'head', axis=1, tiled=True)  60.9 us
    all_to_all x1, waiting for transfers between devices, shards(): lax.all_to_all(jnp.stack([keys_local for _ in range(lax.axis_size('seq'))...  53.1 us
    dot_general x16, matrix products, block_step(): jnp.einsum('hrk,khd->rhd', weights.astype(jnp.bfloat16), value_block, pre...  24.6 us
  transfers between devices with their start and end apart: 8, of which 8 were waited for; matrix products, arithmetic and copies ran while one was open for 2% of the time, Pallas kernels for 0%

profile of v1, /device:TPU:1, one launch (start us, length us, event | category | flops | bytes accessed | tf_op | source)
XLA Modules:
  0.0 601.2 jit_solution(15685094985052655761)
XLA Ops:
  7.9 68.7 %all-gather.7.cloned.1.call-done = bf16[256,2048]{1,0:T(8,128)(2,1)} async-done(((bf16[256,128]{1,0:T(8,128)(2,1)}), bf16[256,2048]{1,0:T(8,128)(2,1)}) %all-gather.7.cloned.1.call-update) | async-done | bytes 1048592 | tf_op jit(solution)/shard_map/all_gather | solution.py:94
  76.6 1.5 convert_reduce_fusion.2
  78.1 1.6 fusion.50
  80.6 1.8 stack.2
  82.5 7.9 %all-to-all-start = ((bf16[32,256,128]{2,1,0:T(8,128)(2,1)}), bf16[32,256,128]{2,1,0:T(8,128)(2,1)}, u32[]{:S(2)}, u32[]{:S(2)}) async-start(bf16[32,256,128]{2,1,0:T(8,128)(2,1)} %stack.2), calls=%async_computation | async-start | bytes 4194304 | tf_op jit(solution)/shard_map/all_to_all | solution.py:107
  92.0 53.1 %all-to-all-done = bf16[32,256,128]{2,1,0:T(8,128)(2,1)} async-done(((bf16[32,256,128]{2,1,0:T(8,128)(2,1)}), bf16[32,256,128]{2,1,0:T(8,128)(2,1)}, u32[]{:S(2)}, u32[]{:S(2)}) %all-to-all-start) | async-done | bytes 2097184 | tf_op jit(solution)/shard_map/all_to_all | solution.py:107
  145.2 22.4 %all-gather.9.cloned.1.call-done = bf16[8192,128]{1,0:T(8,128)(2,1)} async-done(((bf16[256,128]{1,0:T(8,128)(2,1)}), bf16[8192,128]{1,0:T(8,128)(2,1)}) %all-gather.9.cloned.1.call-update) | async-done | bytes 2097168 | tf_op jit(solution)/shard_map/all_gather | solution.py:112
  167.6 29.3 %while.36 = (s32[]{:T(128)}, f32[1,256]{1,0:T(1,128)S(1)}, f32[1,256]{1,0:T(1,128)S(1)}, f32[256,1,128]{0,2,1:T(8,128)S(1)}, s32[]{:T(128)}, /*index=5*/bf16[819...) while((s32[]{:T(128)}, f32[1,256]{1,0:T(1,128)S(1)}, ...), condition=%wide.region_5.6_spmd.clone, body=%wide.region_2.5_spmd.clone.sunk | while | flops 136678656 | bytes 4018367 | solution.py:61
  198.7 89.3 %reduce-scatter.4.cloned.1.call-done = bf16[128,256]{1,0:T(8,128)(2,1)} async-done(((bf16[2048,256]{1,0:T(8,128)(2,1)}), bf16[128,256]{1,0:T(8,128)(2,1)}) %reduce-scatter.4.cloned.1.call-update) | async-done | bytes 65552
  290.3 60.9 %all-gather.11.cloned.1.call-done = bf16[256,2048]{1,0:T(8,128)(2,1)} async-done(((bf16[256,128]{1,0:T(8,128)(2,1)}), bf16[256,2048]{1,0:T(8,128)(2,1)}) %all-gather.11.cloned.1.call-update) | async-done | bytes 1048592 | tf_op jit(solution)/shard_map/all_gather | solution.py:122
  351.1 1.5 convert_reduce_fusion.1
  352.7 1.7 fusion.47
  357.6 62.5 %all-gather.15.cloned.1.call-done = bf16[512,2048]{1,0:T(8,128)(2,1)} async-done(((bf16[512,128]{1,0:T(8,128)(2,1)}), bf16[512,2048]{1,0:T(8,128)(2,1)}) %all-gather.15.cloned.1.call-update) | async-done | bytes 2097168 | tf_op jit(solution)/shard_map/all_gather | solution.py:95
  420.1 2.1 convert_reduce_fusion
  423.9 64.0 %all-gather.17.cloned.1.call-done = bf16[8192,128]{1,0:T(8,128)(2,1)} async-done(((bf16[256,128]{1,0:T(8,128)(2,1)}), bf16[8192,128]{1,0:T(8,128)(2,1)}) %all-gather.17.cloned.1.call-update) | async-done | bytes 2097168 | tf_op jit(solution)/shard_map/all_gather | solution.py:133
  487.9 70.0 %all-gather.13.cloned.1.call-done = bf16[8192,128]{1,0:T(8,128)(2,1)} async-done(((bf16[256,128]{1,0:T(8,128)(2,1)}), bf16[8192,128]{1,0:T(8,128)(2,1)}) %all-gather.13.cloned.1.call-update) | async-done | bytes 2097168 | tf_op jit(solution)/shard_map/all_gather | solution.py:132
  557.9 35.4 %while.37 = (s32[]{:T(128)}, f32[1,512]{1,0:T(1,128)S(1)}, f32[1,512]{1,0:T(1,128)S(1)}, f32[512,1,128]{0,2,1:T(8,128)S(1)}, s32[]{:T(128)}, /*index=5*/bf16[819...) while((s32[]{:T(128)}, f32[1,512]{1,0:T(1,128)S(1)}, ...), condition=%wide.region_14.15_spmd.clone, body=%wide.region_11.14_spmd.clone.sunk | while | flops 275452416 | bytes 7508159 | solution.py:61
  558.5 1.4 fusion.103
  560.6 1.7 fusion.107
  563.0 1.4 fusion.103
  565.0 1.7 fusion.107
  567.4 1.4 fusion.103
  569.5 1.7 fusion.107
  571.9 1.4 fusion.103
  573.9 1.7 fusion.107
  576.3 1.4 fusion.103
  578.3 1.7 fusion.107
  582.8 1.7 fusion.107
  585.1 1.4 fusion.103
  587.2 1.7 fusion.107
  589.6 1.4 fusion.103
  591.6 1.7 fusion.107
  (166 shorter events, 52.6 us)
Async XLA Ops:
  7.2 189.7 %copy-start = (bf16[128,2048]{1,0:T(8,128)(2,1)S(1)}, bf16[128,2048]{1,0:T(8,128)(2,1)}, u32[]{:S(2)}) copy-start(bf16[128,2048]{1,0:T(8,128)(2,1)} %param.26) | copy-start | bytes 1572868
  7.2 72.6 %copy-start.8 = (f32[2048]{0:T(1024)S(1)}, f32[2048]{0:T(1024)}, u32[]{:S(2)}) copy-start(f32[2048]{0:T(1024)} %param.22) | copy-start | bytes 24580
  7.2 69.4 %all-gather.7.cloned.1.call-start = ((), (), s32[]{:S(2)}) async-start(), calls=%async_computation.2 | async-start | bytes 1114112 | tf_op jit(solution)/shard_map/all_gather | solution.py:94
  7.9 72.3 %copy-start.4 = (bf16[2048,128]{1,0:T(8,128)(2,1)S(1)}, bf16[2048,128]{1,0:T(8,128)(2,1)}, u32[]{:S(2)}) copy-start(bf16[2048,128]{1,0:T(8,128)(2,1)} %param.24) | copy-start | bytes 1572868
  76.6 3.2 copy-start.1
  82.5 8.0 %copy-start.5 = (bf16[2048,128]{1,0:T(8,128)(2,1)S(1)}, bf16[2048,128]{1,0:T(8,128)(2,1)}, u32[]{:S(2)}) copy-start(bf16[2048,128]{1,0:T(8,128)(2,1)} %param.25) | copy-start | bytes 1572868
  82.5 9.1 %copy-start.6 = (bf16[2048,128]{1,0:T(8,128)(2,1)S(1)}, bf16[2048,128]{1,0:T(8,128)(2,1)}, u32[]{:S(2)}) copy-start(bf16[2048,128]{1,0:T(8,128)(2,1)} %param.23) | copy-start | bytes 1572868
  82.5 62.7 %all-to-all-start = ((bf16[32,256,128]{2,1,0:T(8,128)(2,1)}), bf16[32,256,128]{2,1,0:T(8,128)(2,1)}, u32[]{:S(2)}, u32[]{:S(2)}) async-start(bf16[32,256,128]{2,1,0:T(8,128)(2,1)} %stack.2), calls=%async_computation | async-start | bytes 4194304 | tf_op jit(solution)/shard_map/all_to_all | solution.py:107
  90.4 77.2 %all-gather.9.cloned.1.call-start = ((), (), s32[]{:S(2)}) async-start(), calls=%async_computation.3 | async-start | bytes 2162688 | tf_op jit(solution)/shard_map/all_gather | solution.py:112
  91.5 196.5 %reduce-scatter.4.cloned.1.call-start = ((), (), s32[]{:S(2)}) async-start(), calls=%async_computation.8 | async-start | bytes 1114112
  196.9 92.1 %copy-start.7 = (bf16[256,128]{1,0:T(8,128)(2,1)S(1)}, bf16[256,128]{1,0:T(8,128)(2,1)}, u32[]{:S(2)}) copy-start(bf16[256,128]{1,0:T(8,128)(2,1)} %param.18) | copy-start | bytes 196612
  198.6 155.8 %copy-start.9 = (bf16[2048,128]{1,0:T(8,128)(2,1)S(1)}, bf16[2048,128]{1,0:T(8,128)(2,1)}, u32[]{:S(2)}) copy-start(bf16[2048,128]{1,0:T(8,128)(2,1)} %param.30) | copy-start | bytes 1572868
  198.6 155.8 %copy-start.12 = (f32[2048]{0:T(1024)S(1)}, f32[2048]{0:T(1024)}, u32[]{:S(2)}) copy-start(f32[2048]{0:T(1024)} %param.27) | copy-start | bytes 24580
  198.7 152.5 %all-gather.11.cloned.1.call-start = ((), (), s32[]{:S(2)}) async-start(), calls=%async_computation.4 | async-start | bytes 1114112 | tf_op jit(solution)/shard_map/all_gather | solution.py:122
  289.6 130.5 %all-gather.15.cloned.1.call-start = ((), (), s32[]{:S(2)}) async-start(), calls=%async_computation.6 | async-start | bytes 2228224 | tf_op jit(solution)/shard_map/all_gather | solution.py:95
  290.2 197.7 %all-gather.17.cloned.1.call-start = ((), (), s32[]{:S(2)}) async-start(), calls=%async_computation.7 | async-start | bytes 2162688 | tf_op jit(solution)/shard_map/all_gather | solution.py:133
  351.1 3.3 copy-start.3
  352.7 3.0 copy-start.10
  355.6 202.2 %all-gather.13.cloned.1.call-start = ((), (), s32[]{:S(2)}) async-start(), calls=%async_computation.5 | async-start | bytes 2162688 | tf_op jit(solution)/shard_map/all_gather | solution.py:132
  420.1 2.2 copy-start.2
  420.1 2.9 copy-start.11
  420.1 2.9 copy-start.13
Sparse Core Ops, SparseCore 0:
  11.0 65.5 all-gather.6
  93.9 73.5 all-gather.8
  198.8 89.1 reduce-scatter.3
  291.8 59.2 all-gather.10
  354.4 65.6 all-gather.14
  422.3 65.5 all-gather.16
  490.8 66.9 all-gather.12
